TPU v7x, 32 devices: a whole 2x2x4 slice. The times are simulated.
32 devices in a mesh: parts: 2 (over x), slab: 8 (over z, y), vblk: 2 (over core).
Axes of the slice: x: 2, y: 2, z: 4, core: 2. Of those that a mesh axis runs over, the one named last changes fastest.
Arguments:
- vectors: float32 [2, 3, 160, 12288], P(None, None, 'vblk', ('parts', 'slab')), parts along dimension 3, may hold values from -6 to 6
- links: float32 [2, 3, 9, 12288], P(None, None, None, ('parts', 'slab')), parts along dimension 3, may hold values from -4 to 4
- rotation: float32 [2, 160, 160], replicated, may hold values from -0.3125 to 0.3125
Outputs:
- rotated: float32 [2, 3, 160, 12288], P(None, None, 'vblk', ('parts', 'slab')), parts along dimension 3
- gram: float32 [4, 160, 160], P('parts', None, 'vblk'), parts along dimension 0
- projected: float32 [4, 160, 160], P('parts', None, 'vblk'), parts along dimension 0
There are 2 independent parts, one for each index of `parts`. A program takes and returns all parts, laid end to end along the dimension named above; an argument that names none is the same for every part. Nothing has to cross between parts.
All inputs are finite; a program needn't handle non-finite values.
Results may differ from a plain program's by a relative error of at most 0.000071.
Values sent between devices are 32-bit elements; how exact they have to be, the bound alone decides.
A program may use at most 192 MiB of HBM per device.

v0:
```python
import functools

import jax
import jax.numpy as jnp
from jax import lax
from jax.experimental import pallas as pl
from jax.experimental.pallas import tpu as pltpu
from jax.sharding import PartitionSpec as P

LX = 96
LY = 4
LZ = 2
GY = 4
LAYER = LY * LX
CHUNK = 16
MESH = pl.DeviceIdType.MESH

center_shift = 8.0
half_width = 6.0
OWN = 6.0 - center_shift


def edge_mask(shape, x):
    lane = lax.broadcasted_iota(jnp.int32, shape, 1)
    mask = lane == x
    for row in range(1, LY):
        mask = mask | (lane == row * LX + x)
    return mask


def x_forward(layer):
    return jnp.where(
        edge_mask(layer.shape, LX - 1),
        pltpu.roll(layer, LX - 1, 1),
        pltpu.roll(layer, LAYER - 1, 1),
    )


def x_backward(layer):
    return jnp.where(
        edge_mask(layer.shape, 0),
        pltpu.roll(layer, LAYER - LX + 1, 1),
        pltpu.roll(layer, 1, 1),
    )


def y_forward(layer, after):
    joined = jnp.concatenate([layer, after], axis=1)
    return pltpu.roll(joined, LAYER + 128 - LX, 1)[:, :LAYER]


def y_backward(layer, before):
    joined = jnp.concatenate([before, layer], axis=1)
    return pltpu.roll(joined, LAYER + LX, 1)[:, :LAYER]


def halves(x):
    high = x.astype(jnp.bfloat16)
    low = (x - high.astype(jnp.float32)).astype(jnp.bfloat16)
    return high, low


def split_dot(left, right, dims):
    dot = functools.partial(
        lax.dot_general, dimension_numbers=(dims, ((), ())), preferred_element_type=jnp.float32
    )
    return dot(left[0], right[0]) + (dot(left[0], right[1]) + dot(left[1], right[0]))


def kernel(
    n, rows, vec_ref, link_ref, turn_ref, out_ref, gram_ref, proj_ref,
    e_v, e_first, e_filt, y_before, y_after, link_y, link_z, spread, moved,
    f_other, b_own, b_other, sums, part, slots, total,
    in_sem, halo_send, halo_recv, link_send, link_recv, pair_send, pair_recv,
    part_send, part_recv, total_send, total_recv,
):
    me = lax.axis_index("slab")
    core = lax.axis_index("vblk")
    count = vec_ref.shape[2]
    chunks = count // CHUNK
    row_pos = lax.rem(me, GY)
    has_up = me + GY < n
    has_down = me >= GY
    has_next = row_pos < GY - 1
    has_prev = row_pos > 0
    fields = (e_v, e_first, e_filt)

    loads = [
        pltpu.make_async_copy(
            vec_ref.at[:, :, :, pl.ds(z * LAYER, LAYER)], e_v.at[:, :, 1 + z], in_sem.at[z]
        )
        for z in range(LZ)
    ]
    for load in loads:
        load.start()

    barrier = pltpu.get_barrier_semaphore()
    pl.semaphore_signal(barrier, inc=1, device_id={"vblk": 1 - core}, device_id_type=MESH)

    def greet(d, carry):
        pl.semaphore_signal(
            barrier, inc=1, device_id={"slab": lax.rem(me + d, n)}, device_id_type=MESH
        )
        return carry

    lax.fori_loop(1, n, greet, 0)

    @pl.when(jnp.logical_not(has_down))
    def _():
        link_z[...] = jnp.zeros_like(link_z)
        for field in fields:
            field[:, :, 0] = jnp.zeros(field.shape[:2] + field.shape[3:], jnp.float32)

    @pl.when(jnp.logical_not(has_up))
    def _():
        for field in fields:
            field[:, :, LZ + 1] = jnp.zeros(field.shape[:2] + field.shape[3:], jnp.float32)

    @pl.when(jnp.logical_not(has_prev))
    def _():
        link_y[...] = jnp.zeros_like(link_y)
        y_before[...] = jnp.zeros_like(y_before)

    @pl.when(jnp.logical_not(has_next))
    def _():
        y_after[...] = jnp.zeros_like(y_after)

    for load in loads:
        load.wait()
    pl.semaphore_wait(barrier, n)

    def halo(stage, kind, chunk):
        field = fields[stage]
        own = pl.ds(pl.multiple_of(chunk * CHUNK, CHUNK), CHUNK)
        src, dst, to = (
            (field.at[:, :, LZ, own], field.at[:, :, 0, own], me + GY),
            (field.at[:, :, 1, own], field.at[:, :, LZ + 1, own], me - GY),
            (
                field.at[:, :, pl.ds(1, LZ), own, pl.ds(0, 128)],
                y_after.at[stage, :, :, :, own],
                me - 1,
            ),
            (
                field.at[:, :, pl.ds(1, LZ), own, pl.ds(LAYER - 128, 128)],
                y_before.at[min(stage, 1), :, :, :, own],
                me + 1,
            ),
        )[kind]
        return pltpu.make_async_remote_copy(
            src_ref=src, dst_ref=dst,
            send_sem=halo_send.at[stage, kind, chunk],
            recv_sem=halo_recv.at[stage, kind, chunk],
            device_id={"slab": to}, device_id_type=MESH,
        )

    sends = (has_up, has_down, has_prev, has_next)
    receives = (has_down, has_up, has_next, has_prev)
    kinds = ((0, 1, 2, 3), (0, 1, 2, 3), (1, 2))

    def start_halo(stage, chunk):
        for kind in kinds[stage]:
            pl.when(sends[kind])(lambda kind=kind: halo(stage, kind, chunk).start())

    def await_halo(stage, chunk):
        for kind in kinds[stage]:
            pl.when(receives[kind])(lambda kind=kind: halo(stage, kind, chunk).wait_recv())

    def link_copy(index):
        if index < LZ:
            src = link_ref.at[1, :, pl.ds((index + 1) * LAYER - 128, 128)]
            dst, to = link_y.at[index], me + 1
        else:
            src = link_ref.at[2, :, pl.ds((LZ - 1) * LAYER, LAYER)]
            dst, to = link_z, me + GY
        return pltpu.make_async_remote_copy(
            src_ref=src, dst_ref=dst, send_sem=link_send.at[index],
            recv_sem=link_recv.at[index], device_id={"slab": to}, device_id_type=MESH,
        )

    def pair_copy(which, chunk):
        own = pl.ds(pl.multiple_of(chunk * CHUNK, CHUNK), CHUNK)
        src = e_filt.at[:, :, pl.ds(1, LZ), own] if which == 0 else b_own.at[:, :, :, own]
        dst = (f_other, b_other)[which].at[:, :, :, own]
        return pltpu.make_async_remote_copy(
            src_ref=src, dst_ref=dst, send_sem=pair_send.at[which, chunk],
            recv_sem=pair_recv.at[which, chunk],
            device_id={"vblk": 1 - core}, device_id_type=MESH,
        )

    def loop(body):
        def step(chunk, carry):
            body(chunk)
            return carry

        lax.fori_loop(0, chunks, step, 0)

    @pl.when(has_next)
    def _():
        for index in range(LZ):
            link_copy(index).start()

    @pl.when(has_up)
    def _():
        link_copy(LZ).start()

    loop(lambda chunk: start_halo(0, chunk))

    @pl.when(has_prev)
    def _():
        for index in range(LZ):
            link_copy(index).wait_recv()

    @pl.when(has_down)
    def _():
        link_copy(LZ).wait_recv()

    for z in range(LZ):
        lanes = pl.ds(z * LAYER, LAYER)
        forward = [link_ref[mu, :, lanes] for mu in range(3)]
        below = link_z[...] if z == 0 else link_ref[2, :, pl.ds((z - 1) * LAYER, LAYER)]
        backward = [x_backward(forward[0]), y_backward(forward[1], link_y[z]), below]
        for side, table in enumerate((forward, backward)):
            for mu in range(3):
                for k in range(18):
                    spread[side, mu, k, z] = jnp.broadcast_to(
                        table[mu][k : k + 1], (8, LAYER)
                    )

    def hop(stage, chunk, finish):
        field = fields[stage]
        both = stage < 2
        own = pl.ds(pl.multiple_of(chunk * CHUNK, CHUNK), CHUNK)

        def shift(z, carry):
            for part_id in range(2):
                for colour in range(3):
                    layer = field[part_id, colour, z + 1, own, :]
                    moved[0, part_id, colour, z] = x_forward(layer)
                    moved[1, part_id, colour, z] = y_forward(
                        layer, y_after[stage, part_id, colour, z, own, :]
                    )
                    if both:
                        moved[2, part_id, colour, z] = x_backward(layer)
                        moved[3, part_id, colour, z] = y_backward(
                            layer, y_before[stage, part_id, colour, z, own, :]
                        )
            return carry

        lax.fori_loop(0, LZ, shift, 0)

        def tile(index, carry):
            z = index // (LAYER // 128)
            lanes = pl.ds(pl.multiple_of(lax.rem(index, LAYER // 128) * 128, 128), 128)

            def take(ref, *at):
                return ref[at].reshape(CHUNK // 8, 8, 128)

            acc_re = [None] * 3
            acc_im = [None] * 3
            for mu in range(3):
                for side in range(2 if both else 1):
                    if mu == 2:
                        here = [
                            take(field, c // 3, c % 3, z + (0 if side else 2), own, lanes)
                            for c in range(6)
                        ]
                    else:
                        here = [
                            take(moved, 2 * side + mu, c // 3, c % 3, z, slice(None), lanes)
                            for c in range(6)
                        ]
                    for row in range(3):
                        for col in range(3):
                            k = row * 3 + col if side == 0 else col * 3 + row
                            link_re = spread[side, mu, k, z, :, lanes]
                            link_im = spread[side, mu, 9 + k, z, :, lanes]
                            re, im = here[col], here[3 + col]
                            if side == 0:
                                real = link_re * re - link_im * im
                                imag = link_re * im + link_im * re
                            else:
                                real = link_re * re + link_im * im
                                imag = link_re * im - link_im * re
                            if acc_re[row] is None:
                                acc_re[row], acc_im[row] = real, imag
                            else:
                                acc_re[row] = acc_re[row] + real
                                acc_im[row] = acc_im[row] + imag
            for row in range(3):
                for part_id, value in ((0, acc_re[row]), (1, acc_im[row])):
                    finish(part_id, row, z, own, lanes, value)
            return carry

        lax.fori_loop(0, LZ * LAYER // 128, tile, 0)

    def merged(ref, part_id, row, z, own, lanes):
        return ref[part_id, row, z, own, lanes].reshape(CHUNK // 8, 8, 128)

    def finish_first(part_id, row, z, own, lanes, value):
        center = merged(e_v, part_id, row, z + 1, own, lanes)
        done = (OWN * center - value) * (1.0 / half_width)
        e_first[part_id, row, z + 1, own, lanes] = done.reshape(CHUNK, 128)

    def finish_filtered(part_id, row, z, own, lanes, value):
        center = merged(e_first, part_id, row, z + 1, own, lanes)
        start = merged(e_v, part_id, row, z + 1, own, lanes)
        done = (OWN * center - value) * (2.0 / half_width) - start
        e_filt[part_id, row, z + 1, own, lanes] = done.reshape(CHUNK, 128)

    def finish_bonds(part_id, row, z, own, lanes, value):
        b_own[part_id, row, z, own, lanes] = value.reshape(CHUNK, 128)

    def do_first(chunk):
        await_halo(0, chunk)
        hop(0, chunk, finish_first)
        start_halo(1, chunk)

    def do_filtered(chunk):
        await_halo(1, chunk)
        hop(1, chunk, finish_filtered)
        pair_copy(0, chunk).start()
        start_halo(2, chunk)

    def do_bonds(chunk):
        await_halo(2, chunk)
        hop(2, chunk, finish_bonds)
        pair_copy(1, chunk).start()

    loop(do_first)
    loop(do_filtered)
    loop(lambda chunk: pair_copy(0, chunk).wait_recv())

    def stacked(ref, colour, z):
        return halves(jnp.concatenate([ref[0, colour, z], ref[1, colour, z]], axis=0))

    lane_dims = ((1,), (1,))
    sums[...] = jnp.zeros_like(sums)
    turn = [halves(turn_ref[side]) for side in range(2)]

    for colour in range(3):
        for z in range(LZ):
            mine = stacked(e_filt, colour, z + 1)
            other = stacked(f_other, colour, z)
            sums[0] += split_dot(mine, mine, lane_dims)
            sums[1] += split_dot(other, mine, lane_dims)
            turned = split_dot(turn[0], mine, ((1,), (0,)))
            turned = turned + split_dot(turn[1], other, ((1,), (0,)))
            for part_id in range(2):
                out_ref[part_id, colour, :, pl.ds(z * LAYER, LAYER)] = turned[
                    part_id * count : (part_id + 1) * count
                ]

    loop(do_bonds)
    loop(lambda chunk: pair_copy(1, chunk).wait_recv())

    for colour in range(3):
        for z in range(LZ):
            mine = stacked(e_filt, colour, z + 1)
            other = stacked(f_other, colour, z)
            bond = stacked(b_own, colour, z)
            bond_other = stacked(b_other, colour, z)
            sums[2] += split_dot(mine, bond, lane_dims) + split_dot(bond, mine, lane_dims)
            sums[3] += split_dot(other, bond, lane_dims) + split_dot(bond_other, mine, lane_dims)

    def inner(index):
        top = sums[index, pl.ds(0, count), :]
        low = sums[index, pl.ds(count, count), :]
        return (
            top[:, :count] + low[:, count:],
            top[:, count:] - low[:, :count],
        )

    sites = 3.0 * n * vec_ref.shape[3]
    fill = jnp.zeros((count, 128 - count), jnp.float32)
    for side, at in ((0, core), (1, 1 - core)):
        gram = inner(side)
        hopped = inner(2 + side)
        for part_id in range(2):
            projected = (OWN * gram[part_id] - hopped[part_id]) * (1.0 / half_width)
            for base, value in ((0, gram[part_id]), (2, projected)):
                first_row = pl.multiple_of((base + part_id) * 2 * count + at * count, 8)
                part[pl.ds(first_row, count), :] = jnp.concatenate(
                    [value * (1.0 / sites), fill], axis=1
                )

    owners = part.shape[0] // rows

    def rows_of(owner):
        return pl.ds(pl.multiple_of(owner * rows, 8), rows)

    def part_copy(d):
        owner = lax.rem(me + d, n)
        return owner, pltpu.make_async_remote_copy(
            src_ref=part.at[rows_of(jnp.minimum(owner, owners - 1))],
            dst_ref=slots.at[d], send_sem=part_send.at[d], recv_sem=part_recv.at[d],
            device_id={"slab": owner}, device_id_type=MESH,
        )

    def total_copy(d):
        source = jnp.minimum(me, owners - 1)
        return pltpu.make_async_remote_copy(
            src_ref=total.at[rows_of(source)], dst_ref=total.at[rows_of(source)],
            send_sem=total_send.at[d], recv_sem=total_recv.at[d],
            device_id={"slab": lax.rem(me + d, n)}, device_id_type=MESH,
        )

    def total_arrival(d):
        source = lax.rem(me + n - d, n)
        where = rows_of(jnp.minimum(source, owners - 1))
        return source, pltpu.make_async_remote_copy(
            src_ref=total.at[where], dst_ref=total.at[where],
            send_sem=total_send.at[d], recv_sem=total_recv.at[d],
            device_id={"slab": lax.rem(me + d, n)}, device_id_type=MESH,
        )

    def around(body):
        def step(d, carry):
            body(d)
            return carry

        lax.fori_loop(1, n, step, 0)

    def send_part(d):
        owner, copy = part_copy(d)
        pl.when(owner < owners)(copy.start)

    def end_part(d):
        owner, copy = part_copy(d)
        pl.when(owner < owners)(copy.wait_send)

    around(send_part)

    @pl.when(me < owners)
    def _():
        mine = rows_of(jnp.minimum(me, owners - 1))
        around(lambda d: part_copy(d)[1].wait_recv())
        total[mine, :] = lax.fori_loop(
            1, n, lambda d, running: running + slots[d], part[mine, :]
        )
        around(lambda d: total_copy(d).start())

    def end_total(d):
        source, copy = total_arrival(d)
        pl.when(source < owners)(copy.wait_recv)

    around(end_total)
    for ref, base in ((gram_ref, 0), (proj_ref, 2)):
        for part_id in range(2):
            ref[part_id] = total[
                pl.ds((base + part_id) * 2 * count, 2 * count), pl.ds(0, count)
            ]

    def end_sends(chunk):
        for stage in range(3):
            for kind in kinds[stage]:
                pl.when(sends[kind])(
                    lambda stage=stage, kind=kind: halo(stage, kind, chunk).wait_send()
                )
        for which in range(2):
            pair_copy(which, chunk).wait_send()

    loop(end_sends)

    @pl.when(has_next)
    def _():
        for index in range(LZ):
            link_copy(index).wait_send()

    @pl.when(has_up)
    def _():
        link_copy(LZ).wait_send()

    around(end_part)

    @pl.when(me < owners)
    def _():
        around(lambda d: total_copy(d).wait_send())


def per_device(n, vectors, links, rotation):
    count, local_sites = vectors.shape[2], vectors.shape[3]
    core = lax.axis_index("vblk")
    link_rows = links.reshape(2, 3, 3, 3, local_sites)
    link_rows = jnp.transpose(link_rows, (2, 0, 1, 3, 4)).reshape(3, 18, local_sites)
    columns = lax.dynamic_slice_in_dim(rotation, core * count, count, 2)
    columns = jnp.swapaxes(columns, 1, 2)
    blocks = []
    for side in (core, 1 - core):
        own = lax.dynamic_slice_in_dim(columns, side * count, count, 2)
        top = jnp.concatenate([own[0], -own[1]], axis=1)
        low = jnp.concatenate([own[1], own[0]], axis=1)
        blocks.append(jnp.concatenate([top, low], axis=0))
    turn = jnp.stack(blocks)

    chunks = count // CHUNK
    all_rows = 4 * 2 * count
    rows = -(-all_rows // n)
    while all_rows % rows or rows % 8:
        rows += 1
    f32 = jnp.float32
    halo_shape = (2, 3, LZ + 2, count, LAYER)
    block = (2, 3, LZ, count, LAYER)
    vmem = pl.BlockSpec(memory_space=pltpu.VMEM)
    return pl.pallas_call(
        functools.partial(kernel, n, rows),
        out_shape=(
            jax.ShapeDtypeStruct(vectors.shape, f32),
            jax.ShapeDtypeStruct((2, 2 * count, count), f32),
            jax.ShapeDtypeStruct((2, 2 * count, count), f32),
        ),
        in_specs=[pl.BlockSpec(memory_space=pl.ANY), vmem, vmem],
        out_specs=(vmem, vmem, vmem),
        scratch_shapes=[
            pltpu.VMEM(halo_shape, f32),
            pltpu.VMEM(halo_shape, f32),
            pltpu.VMEM(halo_shape, f32),
            pltpu.VMEM((2, 2, 3, LZ, count, 128), f32),
            pltpu.VMEM((3, 2, 3, LZ, count, 128), f32),
            pltpu.VMEM((LZ, 18, 128), f32),
            pltpu.VMEM((18, LAYER), f32),
            pltpu.VMEM((2, 3, 18, LZ, 8, LAYER), f32),
            pltpu.VMEM((4, 2, 3, LZ, CHUNK, LAYER), f32),
            pltpu.VMEM(block, f32),
            pltpu.VMEM(block, f32),
            pltpu.VMEM(block, f32),
            pltpu.VMEM((4, 2 * count, 2 * count), f32),
            pltpu.VMEM((all_rows, 128), f32),
            pltpu.VMEM((n, rows, 128), f32),
            pltpu.VMEM((all_rows, 128), f32),
            pltpu.SemaphoreType.DMA((LZ,)),
            pltpu.SemaphoreType.DMA((3, 4, chunks)),
            pltpu.SemaphoreType.DMA((3, 4, chunks)),
            pltpu.SemaphoreType.DMA((LZ + 1,)),
            pltpu.SemaphoreType.DMA((LZ + 1,)),
            pltpu.SemaphoreType.DMA((2, chunks)),
            pltpu.SemaphoreType.DMA((2, chunks)),
            pltpu.SemaphoreType.DMA((n,)),
            pltpu.SemaphoreType.DMA((n,)),
            pltpu.SemaphoreType.DMA((n,)),
            pltpu.SemaphoreType.DMA((n,)),
        ],
        compiler_params=pltpu.CompilerParams(
            collective_id=0, has_side_effects=True, vmem_limit_bytes=56 * 1024 * 1024
        ),
    )(vectors, link_rows, turn)


def solution(mesh):
    in_specs = (
        P(None, None, "vblk", ("parts", "slab")),
        P(None, None, None, ("parts", "slab")),
        P(),
    )
    out_specs = (
        P(None, None, "vblk", ("parts", "slab")),
        P("parts", None, "vblk"),
        P("parts", None, "vblk"),
    )
    return jax.shard_map(
        functools.partial(per_device, mesh.shape["slab"]),
        mesh=mesh, in_specs=in_specs, out_specs=out_specs, check_vma=False,
    )
```

profile of v0, /device:TPU:0, one launch (start us, length us, event | category | flops | bytes accessed | tf_op | source)
XLA Modules:
  0.0 136.8 jit_solution(13476823058482602693)
XLA Ops:
  0.6 0.0 copy-start
  0.6 1.2 constant_dynamic-slice_fusion.1
  1.8 0.1 copy.13
  1.9 0.1 copy.14
  2.0 0.2 maximum_bitcast_fusion
  2.2 0.7 pad_maximum_fusion.turn_ref
  3.0 0.0 copy-done
  3.0 0.1 copy.9
  3.0 0.7 copy.12.link_ref
  3.7 129.0 %shard_map.58 = (f32[2,3,80,768]{3,2,1,0:T(8,128)}, f32[2,160,80]{2,1,0:T(8,128)}, f32[2,160,80]{2,1,0:T(8,128)}) custom-call(f32[2,3,80,768]{3,2,1,0:T(8,128)} %vec_ref.1, f32[3,18,768]{2,1,0:T(8,128)} %copy.12.link_ref, f32[2,160,160]{2,1,0:T(8,128)} %pad_maximum_fusion.turn_ref), custom_call_target="tpu_custom_call" | custom-call | tf_op jit(solution)/shard_map/pallas_call | solution.py:504
  132.8 0.0 copy-start.2
  132.8 0.0 copy-start.1
  132.8 2.6 %copy.18 = f32[2,3,80,768]{3,2,1,0:T(8,128)} copy(f32[2,3,80,768]{3,2,1,0:T(8,128)} %get-tuple-element.14) | data formatting | bytes 2949120
  135.4 0.0 copy-done.2
  135.4 0.7 copy.19
  136.1 0.0 copy-done.1
  136.1 0.7 copy.20
  (4 shorter events, 0.0 us)
Async XLA Ops:
  0.6 2.3 %copy-start = (f32[2,3,9,768]{3,0,2,1:T(2,128)S(1)}, f32[2,3,9,768]{3,0,2,1:T(2,128)}, u32[]{:S(2)}) copy-start(f32[2,3,9,768]{3,0,2,1:T(2,128)} %param.4) | copy-start | bytes 497668
  132.8 2.6 %copy-start.2 = (f32[2,160,80]{2,1,0:T(8,128)S(1)}, f32[2,160,80]{2,1,0:T(8,128)}, u32[]{:S(2)}) copy-start(f32[2,160,80]{2,1,0:T(8,128)} %get-tuple-element.15) | copy-start | bytes 307204
  132.8 3.3 %copy-start.1 = (f32[2,160,80]{2,1,0:T(8,128)S(1)}, f32[2,160,80]{2,1,0:T(8,128)}, u32[]{:S(2)}) copy-start(f32[2,160,80]{2,1,0:T(8,128)} %get-tuple-element.16) | copy-start | bytes 307204
where the time goes:
time: 137 us
  Pallas kernels  129 us (94%)
  local copies, waits for them, and re-layouts  6.09 us (4%)
    pallas_call x1, Pallas kernels, per_device(): pl.pallas_call(functools.partial(kernel, n, rows), out_shape=(jax.ShapeDt...  129 us
    unnamed x11, local copies, waits for them, and re-layouts  4.13 us

commit v1 on v0

--- a/solution.py
+++ b/solution.py
@@ -84,6 +84,8 @@
     has_next = row_pos < GY - 1
     has_prev = row_pos > 0
     fields = (e_v, e_first, e_filt)
+    low_rows = row_pos < GY // 2
+    high_rows = jnp.logical_not(low_rows)
 
     loads = [
         pltpu.make_async_copy(
@@ -108,12 +110,15 @@
     @pl.when(jnp.logical_not(has_down))
     def _():
         link_z[...] = jnp.zeros_like(link_z)
-        for field in fields:
+        for field in fields[:2]:
             field[:, :, 0] = jnp.zeros(field.shape[:2] + field.shape[3:], jnp.float32)
 
+    for edge in (0, LZ + 1):
+        e_filt[:, :, edge] = jnp.zeros(e_filt.shape[:2] + e_filt.shape[3:], jnp.float32)
+
     @pl.when(jnp.logical_not(has_up))
     def _():
-        for field in fields:
+        for field in fields[:2]:
             field[:, :, LZ + 1] = jnp.zeros(field.shape[:2] + field.shape[3:], jnp.float32)
 
     @pl.when(jnp.logical_not(has_prev))
@@ -132,9 +137,12 @@
     def halo(stage, kind, chunk):
         field = fields[stage]
         own = pl.ds(pl.multiple_of(chunk * CHUNK, CHUNK), CHUNK)
+        up = pl.ds(LAYER - 128, 128) if stage == 2 else slice(None)
+        down = pl.ds(0, 128) if stage == 2 else slice(None)
+        middle = pl.ds(128, 128)
         src, dst, to = (
-            (field.at[:, :, LZ, own], field.at[:, :, 0, own], me + GY),
-            (field.at[:, :, 1, own], field.at[:, :, LZ + 1, own], me - GY),
+            (field.at[:, :, LZ, own, up], field.at[:, :, 0, own, up], me + GY),
+            (field.at[:, :, 1, own, down], field.at[:, :, LZ + 1, own, down], me - GY),
             (
                 field.at[:, :, pl.ds(1, LZ), own, pl.ds(0, 128)],
                 y_after.at[stage, :, :, :, own],
@@ -145,6 +153,8 @@
                 y_before.at[min(stage, 1), :, :, :, own],
                 me + 1,
             ),
+            (field.at[:, :, LZ, own, middle], field.at[:, :, 0, own, middle], me + GY),
+            (field.at[:, :, 1, own, middle], field.at[:, :, LZ + 1, own, middle], me - GY),
         )[kind]
         return pltpu.make_async_remote_copy(
             src_ref=src, dst_ref=dst,
@@ -153,9 +163,9 @@
             device_id={"slab": to}, device_id_type=MESH,
         )
 
-    sends = (has_up, has_down, has_prev, has_next)
-    receives = (has_down, has_up, has_next, has_prev)
-    kinds = ((0, 1, 2, 3), (0, 1, 2, 3), (1, 2))
+    sends = (has_up, has_down, has_prev, has_next, has_up & high_rows, has_down & low_rows)
+    receives = (has_down, has_up, has_next, has_prev, has_down & high_rows, has_up & low_rows)
+    kinds = ((0, 1, 2, 3), (0, 1, 2, 3), (0, 1, 4, 5, 2))
 
     def start_halo(stage, chunk):
         for kind in kinds[stage]:
@@ -248,50 +258,65 @@
 
         lax.fori_loop(0, LZ, shift, 0)
 
+        def take(ref, *at):
+            return ref[at].reshape(CHUNK // 8, 8, 128)
+
+        def add_hops(pairs, z, lanes):
+            acc_re = [None] * 3
+            acc_im = [None] * 3
+            for mu, side in pairs:
+                if mu == 2:
+                    here = [
+                        take(field, c // 3, c % 3, z + (0 if side else 2), own, lanes)
+                        for c in range(6)
+                    ]
+                else:
+                    here = [
+                        take(moved, 2 * side + mu, c // 3, c % 3, z, slice(None), lanes)
+                        for c in range(6)
+                    ]
+                for row in range(3):
+                    for col in range(3):
+                        k = row * 3 + col if side == 0 else col * 3 + row
+                        link_re = spread[side, mu, k, z, :, lanes]
+                        link_im = spread[side, mu, 9 + k, z, :, lanes]
+                        re, im = here[col], here[3 + col]
+                        if side == 0:
+                            real = link_re * re - link_im * im
+                            imag = link_re * im + link_im * re
+                        else:
+                            real = link_re * re + link_im * im
+                            imag = link_re * im - link_im * re
+                        if acc_re[row] is None:
+                            acc_re[row], acc_im[row] = real, imag
+                        else:
+                            acc_re[row] = acc_re[row] + real
+                            acc_im[row] = acc_im[row] + imag
+            return acc_re, acc_im
+
         def tile(index, carry):
             z = index // (LAYER // 128)
             lanes = pl.ds(pl.multiple_of(lax.rem(index, LAYER // 128) * 128, 128), 128)
-
-            def take(ref, *at):
-                return ref[at].reshape(CHUNK // 8, 8, 128)
-
-            acc_re = [None] * 3
-            acc_im = [None] * 3
-            for mu in range(3):
-                for side in range(2 if both else 1):
-                    if mu == 2:
-                        here = [
-                            take(field, c // 3, c % 3, z + (0 if side else 2), own, lanes)
-                            for c in range(6)
-                        ]
-                    else:
-                        here = [
-                            take(moved, 2 * side + mu, c // 3, c % 3, z, slice(None), lanes)
-                            for c in range(6)
-                        ]
-                    for row in range(3):
-                        for col in range(3):
-                            k = row * 3 + col if side == 0 else col * 3 + row
-                            link_re = spread[side, mu, k, z, :, lanes]
-                            link_im = spread[side, mu, 9 + k, z, :, lanes]
-                            re, im = here[col], here[3 + col]
-                            if side == 0:
-                                real = link_re * re - link_im * im
-                                imag = link_re * im + link_im * re
-                            else:
-                                real = link_re * re + link_im * im
-                                imag = link_re * im - link_im * re
-                            if acc_re[row] is None:
-                                acc_re[row], acc_im[row] = real, imag
-                            else:
-                                acc_re[row] = acc_re[row] + real
-                                acc_im[row] = acc_im[row] + imag
+            sides = (0, 1) if both else (0,)
+            pairs = [(mu, side) for mu in range(3) for side in sides]
+            sums_of = add_hops(pairs, z, lanes)
             for row in range(3):
-                for part_id, value in ((0, acc_re[row]), (1, acc_im[row])):
-                    finish(part_id, row, z, own, lanes, value)
+                for part_id in range(2):
+                    finish(part_id, row, z, own, lanes, sums_of[part_id][row])
             return carry
 
+        def edge_tile(index, carry):
+            lanes = pl.ds(pl.multiple_of(index * 128, 128), 128)
+            sums_of = add_hops([(2, 1)], 0, lanes)
+            for row in range(3):
+                for part_id in range(2):
+                    there = merged(b_own, part_id, row, 0, own, lanes)
+                    finish(part_id, row, 0, own, lanes, there + sums_of[part_id][row])
+            return carry
+
         lax.fori_loop(0, LZ * LAYER // 128, tile, 0)
+        if not both:
+            lax.fori_loop(0, LAYER // 128, edge_tile, 0)
 
     def merged(ref, part_id, row, z, own, lanes):
         return ref[part_id, row, z, own, lanes].reshape(CHUNK // 8, 8, 128)
@@ -371,48 +396,42 @@
         )
 
     sites = 3.0 * n * vec_ref.shape[3]
-    fill = jnp.zeros((count, 128 - count), jnp.float32)
-    for side, at in ((0, core), (1, 1 - core)):
+    spare = 128 - count
+    full = 8 * count // 128
+    blocks = []
+    for side in range(2):
         gram = inner(side)
         hopped = inner(2 + side)
         for part_id in range(2):
             projected = (OWN * gram[part_id] - hopped[part_id]) * (1.0 / half_width)
-            for base, value in ((0, gram[part_id]), (2, projected)):
-                first_row = pl.multiple_of((base + part_id) * 2 * count + at * count, 8)
-                part[pl.ds(first_row, count), :] = jnp.concatenate(
-                    [value * (1.0 / sites), fill], axis=1
-                )
-
-    owners = part.shape[0] // rows
+            blocks += [gram[part_id] * (1.0 / sites), projected * (1.0 / sites)]
+    tail = jnp.concatenate(blocks[full:], axis=1)
+    for index in range(full):
+        part[pl.ds(index * count, count), :] = jnp.concatenate(
+            [blocks[index], tail[:, index * spare : (index + 1) * spare]], axis=1
+        )
+    if part.shape[0] > full * count:
+        left = part.shape[0] - full * count
+        part[pl.ds(full * count, left), :] = jnp.zeros((left, 128), jnp.float32)
 
     def rows_of(owner):
         return pl.ds(pl.multiple_of(owner * rows, 8), rows)
 
     def part_copy(d):
         owner = lax.rem(me + d, n)
-        return owner, pltpu.make_async_remote_copy(
-            src_ref=part.at[rows_of(jnp.minimum(owner, owners - 1))],
+        return pltpu.make_async_remote_copy(
+            src_ref=part.at[rows_of(owner)],
             dst_ref=slots.at[d], send_sem=part_send.at[d], recv_sem=part_recv.at[d],
             device_id={"slab": owner}, device_id_type=MESH,
         )
 
-    def total_copy(d):
-        source = jnp.minimum(me, owners - 1)
+    def total_copy(d, source):
         return pltpu.make_async_remote_copy(
             src_ref=total.at[rows_of(source)], dst_ref=total.at[rows_of(source)],
             send_sem=total_send.at[d], recv_sem=total_recv.at[d],
             device_id={"slab": lax.rem(me + d, n)}, device_id_type=MESH,
         )
 
-    def total_arrival(d):
-        source = lax.rem(me + n - d, n)
-        where = rows_of(jnp.minimum(source, owners - 1))
-        return source, pltpu.make_async_remote_copy(
-            src_ref=total.at[where], dst_ref=total.at[where],
-            send_sem=total_send.at[d], recv_sem=total_recv.at[d],
-            device_id={"slab": lax.rem(me + d, n)}, device_id_type=MESH,
-        )
-
     def around(body):
         def step(d, carry):
             body(d)
@@ -420,35 +439,23 @@
 
         lax.fori_loop(1, n, step, 0)
 
-    def send_part(d):
-        owner, copy = part_copy(d)
-        pl.when(owner < owners)(copy.start)
-
-    def end_part(d):
-        owner, copy = part_copy(d)
-        pl.when(owner < owners)(copy.wait_send)
-
-    around(send_part)
-
-    @pl.when(me < owners)
-    def _():
-        mine = rows_of(jnp.minimum(me, owners - 1))
-        around(lambda d: part_copy(d)[1].wait_recv())
-        total[mine, :] = lax.fori_loop(
-            1, n, lambda d, running: running + slots[d], part[mine, :]
-        )
-        around(lambda d: total_copy(d).start())
-
-    def end_total(d):
-        source, copy = total_arrival(d)
-        pl.when(source < owners)(copy.wait_recv)
-
-    around(end_total)
-    for ref, base in ((gram_ref, 0), (proj_ref, 2)):
+    around(lambda d: part_copy(d).start())
+    around(lambda d: part_copy(d).wait_recv())
+    total[rows_of(me), :] = lax.fori_loop(
+        1, n, lambda d, running: running + slots[d], part[rows_of(me), :]
+    )
+    around(lambda d: total_copy(d, me).start())
+    around(lambda d: total_copy(d, lax.rem(me + n - d, n)).wait_recv())
+
+    packed = [total[pl.ds(index * count, count), :] for index in range(full)]
+    tail = jnp.concatenate([block[:, count:] for block in packed], axis=1)
+    found = [block[:, :count] for block in packed]
+    found += [tail[:, i * count : (i + 1) * count] for i in range(8 - full)]
+    for side, at in ((0, core), (1, 1 - core)):
+        own_rows = pl.ds(pl.multiple_of(at * count, 8), count)
         for part_id in range(2):
-            ref[part_id] = total[
-                pl.ds((base + part_id) * 2 * count, 2 * count), pl.ds(0, count)
-            ]
+            gram_ref[part_id, own_rows, :] = found[4 * side + 2 * part_id]
+            proj_ref[part_id, own_rows, :] = found[4 * side + 2 * part_id + 1]
 
     def end_sends(chunk):
         for stage in range(3):
@@ -470,11 +477,8 @@
     def _():
         link_copy(LZ).wait_send()
 
-    around(end_part)
-
-    @pl.when(me < owners)
-    def _():
-        around(lambda d: total_copy(d).wait_send())
+    around(lambda d: part_copy(d).wait_send())
+    around(lambda d: total_copy(d, me).wait_send())
 
 
 def per_device(n, vectors, links, rotation):
@@ -493,10 +497,8 @@
     turn = jnp.stack(blocks)
 
     chunks = count // CHUNK
-    all_rows = 4 * 2 * count
-    rows = -(-all_rows // n)
-    while all_rows % rows or rows % 8:
-        rows += 1
+    rows = 8 * -(-8 * count * count // (128 * 8 * n))
+    all_rows = n * rows
     f32 = jnp.float32
     halo_shape = (2, 3, LZ + 2, count, LAYER)
     block = (2, 3, LZ, count, LAYER)
@@ -528,8 +530,8 @@
             pltpu.VMEM((n, rows, 128), f32),
             pltpu.VMEM((all_rows, 128), f32),
             pltpu.SemaphoreType.DMA((LZ,)),
-            pltpu.SemaphoreType.DMA((3, 4, chunks)),
-            pltpu.SemaphoreType.DMA((3, 4, chunks)),
+            pltpu.SemaphoreType.DMA((3, 6, chunks)),
+            pltpu.SemaphoreType.DMA((3, 6, chunks)),
             pltpu.SemaphoreType.DMA((LZ + 1,)),
             pltpu.SemaphoreType.DMA((LZ + 1,)),
             pltpu.SemaphoreType.DMA((2, chunks)),

time: 137 us -> 118 us (0.86)
  Pallas kernels: 129 us -> 110 us
    pallas_call x1, Pallas kernels: 129 us -> 110 us  [per_device(): pl.pallas_call(functools.partial(kernel, n, rows), out_shape=(jax.ShapeDt...]
where the time goes in v1:
time: 118 us
  Pallas kernels  110 us (93%)
  local copies, waits for them, and re-layouts  6.09 us (5%)
    pallas_call x1, Pallas kernels, per_device(): pl.pallas_call(functools.partial(kernel, n, rows), out_shape=(jax.ShapeDt...  110 us
    unnamed x11, local copies, waits for them, and re-layouts  4.13 us

profile of v1, /device:TPU:0, one launch (start us, length us, event | category | flops | bytes accessed | tf_op | source)
XLA Modules:
  0.0 117.9 jit_solution(12821333268629812258)
XLA Ops:
  0.6 0.0 copy-start
  0.6 1.2 constant_dynamic-slice_fusion.1
  1.8 0.1 copy.13
  1.9 0.1 copy.14
  2.0 0.2 maximum_bitcast_fusion
  2.2 0.7 pad_maximum_fusion.turn_ref
  3.0 0.0 copy-done
  3.0 0.1 copy.9
  3.0 0.7 copy.12.link_ref
  3.7 110.2 %shard_map.58 = (f32[2,3,80,768]{3,2,1,0:T(8,128)}, f32[2,160,80]{2,1,0:T(8,128)}, f32[2,160,80]{2,1,0:T(8,128)}) custom-call(f32[2,3,80,768]{3,2,1,0:T(8,128)} %vec_ref.1, f32[3,18,768]{2,1,0:T(8,128)} %copy.12.link_ref, f32[2,160,160]{2,1,0:T(8,128)} %pad_maximum_fusion.turn_ref), custom_call_target="tpu_custom_call" | custom-call | tf_op jit(solution)/shard_map/pallas_call | solution.py:506
  113.9 0.0 copy-start.2
  114.0 0.0 copy-start.1
  114.0 2.6 %copy.18 = f32[2,3,80,768]{3,2,1,0:T(8,128)} copy(f32[2,3,80,768]{3,2,1,0:T(8,128)} %get-tuple-element.14) | data formatting | bytes 2949120
  116.6 0.0 copy-done.2
  116.6 0.7 copy.19
  117.3 0.0 copy-done.1
  117.3 0.7 copy.20
  (4 shorter events, 0.0 us)
Async XLA Ops:
  0.6 2.3 %copy-start = (f32[2,3,9,768]{3,0,2,1:T(2,128)S(1)}, f32[2,3,9,768]{3,0,2,1:T(2,128)}, u32[]{:S(2)}) copy-start(f32[2,3,9,768]{3,0,2,1:T(2,128)} %param.4) | copy-start | bytes 497668
  113.9 2.6 %copy-start.2 = (f32[2,160,80]{2,1,0:T(8,128)S(1)}, f32[2,160,80]{2,1,0:T(8,128)}, u32[]{:S(2)}) copy-start(f32[2,160,80]{2,1,0:T(8,128)} %get-tuple-element.15) | copy-start | bytes 307204
  114.0 3.3 %copy-start.1 = (f32[2,160,80]{2,1,0:T(8,128)S(1)}, f32[2,160,80]{2,1,0:T(8,128)}, u32[]{:S(2)}) copy-start(f32[2,160,80]{2,1,0:T(8,128)} %get-tuple-element.16) | copy-start | bytes 307204

commit v2 on v1

--- a/solution.py
+++ b/solution.py
@@ -68,11 +68,11 @@
 
 
 def kernel(
-    n, rows, vec_ref, link_ref, turn_ref, out_ref, gram_ref, proj_ref,
+    n, rows, vec_ref, raw_ref, turn_ref, result_ref, gram_ref, proj_ref,
     e_v, e_first, e_filt, y_before, y_after, link_y, link_z, spread, moved,
     f_other, b_own, b_other, sums, part, slots, total,
     in_sem, halo_send, halo_recv, link_send, link_recv, pair_send, pair_recv,
-    part_send, part_recv, total_send, total_recv,
+    part_send, part_recv, total_send, total_recv, link_ref, columns, out_ref, out_sem,
 ):
     me = lax.axis_index("slab")
     core = lax.axis_index("vblk")
@@ -106,6 +106,14 @@
         return carry
 
     lax.fori_loop(1, n, greet, 0)
+
+    for mu in range(3):
+        for row in range(3):
+            for col in range(3):
+                for c in range(2):
+                    link_ref[mu, pl.ds(9 * c + 3 * row + col, 1), :] = raw_ref[
+                        row, 3 * mu + col, pl.ds(c, 1), :
+                    ]
 
     @pl.when(jnp.logical_not(has_down))
     def _():
@@ -351,6 +359,12 @@
         hop(2, chunk, finish_bonds)
         pair_copy(1, chunk).start()
 
+    for c in range(2):
+
+        @pl.when(core == c)
+        def _(c=c):
+            columns[...] = turn_ref[:, :, pl.ds(c * count, count)]
+
     loop(do_first)
     loop(do_filtered)
     loop(lambda chunk: pair_copy(0, chunk).wait_recv())
@@ -360,7 +374,15 @@
 
     lane_dims = ((1,), (1,))
     sums[...] = jnp.zeros_like(sums)
-    turn = [halves(turn_ref[side]) for side in range(2)]
+    turn = []
+    for at in (core, 1 - core):
+        real, imag = [
+            columns[c, pl.ds(pl.multiple_of(at * count, 8), count), :] for c in range(2)
+        ]
+        left = jnp.concatenate(
+            [jnp.concatenate([real, imag], 1), jnp.concatenate([-imag, real], 1)], 0
+        )
+        turn.append(halves(left))
 
     for colour in range(3):
         for z in range(LZ):
@@ -368,24 +390,32 @@
             other = stacked(f_other, colour, z)
             sums[0] += split_dot(mine, mine, lane_dims)
             sums[1] += split_dot(other, mine, lane_dims)
-            turned = split_dot(turn[0], mine, ((1,), (0,)))
-            turned = turned + split_dot(turn[1], other, ((1,), (0,)))
+            turned = split_dot(turn[0], mine, ((0,), (0,)))
+            turned = turned + split_dot(turn[1], other, ((0,), (0,)))
             for part_id in range(2):
                 out_ref[part_id, colour, :, pl.ds(z * LAYER, LAYER)] = turned[
                     part_id * count : (part_id + 1) * count
                 ]
 
+    result = pltpu.make_async_copy(out_ref, result_ref, out_sem)
+    result.start()
     loop(do_bonds)
-    loop(lambda chunk: pair_copy(1, chunk).wait_recv())
 
     for colour in range(3):
         for z in range(LZ):
             mine = stacked(e_filt, colour, z + 1)
             other = stacked(f_other, colour, z)
             bond = stacked(b_own, colour, z)
+            sums[2] += split_dot(mine, bond, lane_dims) + split_dot(bond, mine, lane_dims)
+            sums[3] += split_dot(other, bond, lane_dims)
+
+    loop(lambda chunk: pair_copy(1, chunk).wait_recv())
+
+    for colour in range(3):
+        for z in range(LZ):
+            mine = stacked(e_filt, colour, z + 1)
             bond_other = stacked(b_other, colour, z)
-            sums[2] += split_dot(mine, bond, lane_dims) + split_dot(bond, mine, lane_dims)
-            sums[3] += split_dot(other, bond, lane_dims) + split_dot(bond_other, mine, lane_dims)
+            sums[3] += split_dot(bond_other, mine, lane_dims)
 
     def inner(index):
         top = sums[index, pl.ds(0, count), :]
@@ -479,23 +509,11 @@
 
     around(lambda d: part_copy(d).wait_send())
     around(lambda d: total_copy(d, me).wait_send())
+    result.wait()
 
 
 def per_device(n, vectors, links, rotation):
     count, local_sites = vectors.shape[2], vectors.shape[3]
-    core = lax.axis_index("vblk")
-    link_rows = links.reshape(2, 3, 3, 3, local_sites)
-    link_rows = jnp.transpose(link_rows, (2, 0, 1, 3, 4)).reshape(3, 18, local_sites)
-    columns = lax.dynamic_slice_in_dim(rotation, core * count, count, 2)
-    columns = jnp.swapaxes(columns, 1, 2)
-    blocks = []
-    for side in (core, 1 - core):
-        own = lax.dynamic_slice_in_dim(columns, side * count, count, 2)
-        top = jnp.concatenate([own[0], -own[1]], axis=1)
-        low = jnp.concatenate([own[1], own[0]], axis=1)
-        blocks.append(jnp.concatenate([top, low], axis=0))
-    turn = jnp.stack(blocks)
-
     chunks = count // CHUNK
     rows = 8 * -(-8 * count * count // (128 * 8 * n))
     all_rows = n * rows
@@ -511,7 +529,7 @@
             jax.ShapeDtypeStruct((2, 2 * count, count), f32),
         ),
         in_specs=[pl.BlockSpec(memory_space=pl.ANY), vmem, vmem],
-        out_specs=(vmem, vmem, vmem),
+        out_specs=(pl.BlockSpec(memory_space=pl.ANY), vmem, vmem),
         scratch_shapes=[
             pltpu.VMEM(halo_shape, f32),
             pltpu.VMEM(halo_shape, f32),
@@ -540,11 +558,15 @@
             pltpu.SemaphoreType.DMA((n,)),
             pltpu.SemaphoreType.DMA((n,)),
             pltpu.SemaphoreType.DMA((n,)),
+            pltpu.VMEM((3, 18, local_sites), f32),
+            pltpu.VMEM((2, 2 * count, count), f32),
+            pltpu.VMEM(vectors.shape, f32),
+            pltpu.SemaphoreType.DMA,
         ],
         compiler_params=pltpu.CompilerParams(
             collective_id=0, has_side_effects=True, vmem_limit_bytes=56 * 1024 * 1024
         ),
-    )(vectors, link_rows, turn)
+    )(vectors, jnp.transpose(links, (1, 2, 0, 3)), rotation)
 
 
 def solution(mesh):

time: 118 us -> 113 us (0.958)
  local copies, waits for them, and re-layouts: 6.09 us -> 3.96 us
  Pallas kernels: 110 us -> 108 us
    pallas_call x1, Pallas kernels: 110 us -> 108 us  [per_device(): pl.pallas_call(functools.partial(kernel, n, rows), out_shape=(jax.ShapeDt...]
    unnamed x11 -> x7, local copies, waits for them, and re-layouts: 4.13 us -> 3.96 us
where the time goes in v2:
time: 113 us
  Pallas kernels  108 us (96%)
  local copies, waits for them, and re-layouts  3.96 us (4%)
    pallas_call x1, Pallas kernels, per_device(): pl.pallas_call(functools.partial(kernel, n, rows), out_shape=(jax.ShapeDt...  108 us
    unnamed x7, local copies, waits for them, and re-layouts  3.96 us

profile of v2, /device:TPU:0, one launch (start us, length us, event | category | flops | bytes accessed | tf_op | source)
XLA Modules:
  0.0 112.7 jit_solution(18058898268054039540)
XLA Ops:
  0.6 108.1 %shard_map.58 = (f32[2,3,80,768]{3,2,1,0:T(8,128)}, f32[2,160,80]{2,1,0:T(8,128)}, f32[2,160,80]{2,1,0:T(8,128)}) custom-call(f32[2,3,80,768]{3,2,1,0:T(8,128)} %vec_ref.1, f32[3,9,2,768]{3,2,1,0:T(2,128)} %bitcast.1, f32[2,160,160]{2,1,0:T(8,128)} %turn_ref.1), custom_call_target="tpu_custom_call" | custom-call | tf_op jit(solution)/shard_map/pallas_call | solution.py:524
  108.7 0.0 copy-start.1
  108.8 0.0 copy-start
  108.8 2.6 %copy.9 = f32[2,3,80,768]{3,2,1,0:T(8,128)} copy(f32[2,3,80,768]{3,2,1,0:T(8,128)} %get-tuple-element.6) | data formatting | bytes 2949120
  111.4 0.0 copy-done.1
  111.4 0.7 copy.10
  112.1 0.0 copy-done
  112.1 0.7 copy.11
Async XLA Ops:
  108.7 2.6 %copy-start.1 = (f32[2,160,80]{2,1,0:T(8,128)S(1)}, f32[2,160,80]{2,1,0:T(8,128)}, u32[]{:S(2)}) copy-start(f32[2,160,80]{2,1,0:T(8,128)} %get-tuple-element.7) | copy-start | bytes 307204
  108.8 3.3 %copy-start = (f32[2,160,80]{2,1,0:T(8,128)S(1)}, f32[2,160,80]{2,1,0:T(8,128)}, u32[]{:S(2)}) copy-start(f32[2,160,80]{2,1,0:T(8,128)} %get-tuple-element.8) | copy-start | bytes 307204

commit v3 on v2

--- a/solution.py
+++ b/solution.py
@@ -397,9 +397,79 @@
                     part_id * count : (part_id + 1) * count
                 ]
 
+    def inner(index):
+        top = sums[index, pl.ds(0, count), :]
+        low = sums[index, pl.ds(count, count), :]
+        return (
+            top[:, :count] + low[:, count:],
+            top[:, count:] - low[:, :count],
+        )
+
+    sites = 3.0 * n * vec_ref.shape[3]
+    spare = 128 - count
+    full = -(-4 * count // 128)
+    proj_blocks = []
+
+    def pack(which, blocks):
+        fill = jnp.zeros((count, full * spare - (4 - full) * count), jnp.float32)
+        tail = jnp.concatenate(blocks[full:] + [fill], axis=1)
+        for index in range(full):
+            part[which, pl.ds(index * count, count), :] = jnp.concatenate(
+                [blocks[index], tail[:, index * spare : (index + 1) * spare]], axis=1
+            )
+        left = part.shape[1] - full * count
+        if left:
+            part[which, pl.ds(full * count, left), :] = jnp.zeros((left, 128), jnp.float32)
+
+    def unpack(which, ref):
+        packed = [total[which, pl.ds(index * count, count), :] for index in range(full)]
+        tail = jnp.concatenate([block[:, count:] for block in packed], axis=1)
+        found = [block[:, :count] for block in packed]
+        found += [tail[:, i * count : (i + 1) * count] for i in range(4 - full)]
+        for side, at in ((0, core), (1, 1 - core)):
+            for part_id in range(2):
+                ref[part_id, pl.ds(pl.multiple_of(at * count, 8), count), :] = found[
+                    2 * side + part_id
+                ]
+
+    def around(body):
+        def step(d, carry):
+            body(d)
+            return carry
+
+        lax.fori_loop(1, n, step, 0)
+
+    def rows_of(owner):
+        return pl.ds(pl.multiple_of(owner * rows, 8), rows)
+
+    def part_copy(which, d):
+        owner = lax.rem(me + d, n)
+        return pltpu.make_async_remote_copy(
+            src_ref=part.at[which, rows_of(owner)], dst_ref=slots.at[which, d],
+            send_sem=part_send.at[which, d], recv_sem=part_recv.at[which, d],
+            device_id={"slab": owner}, device_id_type=MESH,
+        )
+
+    def total_copy(which, d, source):
+        return pltpu.make_async_remote_copy(
+            src_ref=total.at[which, rows_of(source)], dst_ref=total.at[which, rows_of(source)],
+            send_sem=total_send.at[which, d], recv_sem=total_recv.at[which, d],
+            device_id={"slab": lax.rem(me + d, n)}, device_id_type=MESH,
+        )
+
+    def gather_sums(which):
+        around(lambda d: part_copy(which, d).wait_recv())
+        total[which, rows_of(me), :] = lax.fori_loop(
+            1, n, lambda d, running: running + slots[which, d], part[which, rows_of(me), :]
+        )
+        around(lambda d: total_copy(which, d, me).start())
+
     result = pltpu.make_async_copy(out_ref, result_ref, out_sem)
     result.start()
+    pack(0, [value * (1.0 / sites) for side in range(2) for value in inner(side)])
+    around(lambda d: part_copy(0, d).start())
     loop(do_bonds)
+    gather_sums(0)
 
     for colour in range(3):
         for z in range(LZ):
@@ -417,75 +487,18 @@
             bond_other = stacked(b_other, colour, z)
             sums[3] += split_dot(bond_other, mine, lane_dims)
 
-    def inner(index):
-        top = sums[index, pl.ds(0, count), :]
-        low = sums[index, pl.ds(count, count), :]
-        return (
-            top[:, :count] + low[:, count:],
-            top[:, count:] - low[:, :count],
-        )
-
-    sites = 3.0 * n * vec_ref.shape[3]
-    spare = 128 - count
-    full = 8 * count // 128
-    blocks = []
     for side in range(2):
-        gram = inner(side)
-        hopped = inner(2 + side)
+        grams, bonds = inner(side), inner(2 + side)
         for part_id in range(2):
-            projected = (OWN * gram[part_id] - hopped[part_id]) * (1.0 / half_width)
-            blocks += [gram[part_id] * (1.0 / sites), projected * (1.0 / sites)]
-    tail = jnp.concatenate(blocks[full:], axis=1)
-    for index in range(full):
-        part[pl.ds(index * count, count), :] = jnp.concatenate(
-            [blocks[index], tail[:, index * spare : (index + 1) * spare]], axis=1
-        )
-    if part.shape[0] > full * count:
-        left = part.shape[0] - full * count
-        part[pl.ds(full * count, left), :] = jnp.zeros((left, 128), jnp.float32)
-
-    def rows_of(owner):
-        return pl.ds(pl.multiple_of(owner * rows, 8), rows)
-
-    def part_copy(d):
-        owner = lax.rem(me + d, n)
-        return pltpu.make_async_remote_copy(
-            src_ref=part.at[rows_of(owner)],
-            dst_ref=slots.at[d], send_sem=part_send.at[d], recv_sem=part_recv.at[d],
-            device_id={"slab": owner}, device_id_type=MESH,
-        )
-
-    def total_copy(d, source):
-        return pltpu.make_async_remote_copy(
-            src_ref=total.at[rows_of(source)], dst_ref=total.at[rows_of(source)],
-            send_sem=total_send.at[d], recv_sem=total_recv.at[d],
-            device_id={"slab": lax.rem(me + d, n)}, device_id_type=MESH,
-        )
-
-    def around(body):
-        def step(d, carry):
-            body(d)
-            return carry
-
-        lax.fori_loop(1, n, step, 0)
-
-    around(lambda d: part_copy(d).start())
-    around(lambda d: part_copy(d).wait_recv())
-    total[rows_of(me), :] = lax.fori_loop(
-        1, n, lambda d, running: running + slots[d], part[rows_of(me), :]
-    )
-    around(lambda d: total_copy(d, me).start())
-    around(lambda d: total_copy(d, lax.rem(me + n - d, n)).wait_recv())
-
-    packed = [total[pl.ds(index * count, count), :] for index in range(full)]
-    tail = jnp.concatenate([block[:, count:] for block in packed], axis=1)
-    found = [block[:, :count] for block in packed]
-    found += [tail[:, i * count : (i + 1) * count] for i in range(8 - full)]
-    for side, at in ((0, core), (1, 1 - core)):
-        own_rows = pl.ds(pl.multiple_of(at * count, 8), count)
-        for part_id in range(2):
-            gram_ref[part_id, own_rows, :] = found[4 * side + 2 * part_id]
-            proj_ref[part_id, own_rows, :] = found[4 * side + 2 * part_id + 1]
+            projected = (OWN * grams[part_id] - bonds[part_id]) * (1.0 / half_width)
+            proj_blocks.append(projected * (1.0 / sites))
+    pack(1, proj_blocks)
+    around(lambda d: part_copy(1, d).start())
+    around(lambda d: total_copy(0, d, lax.rem(me + n - d, n)).wait_recv())
+    unpack(0, gram_ref)
+    gather_sums(1)
+    around(lambda d: total_copy(1, d, lax.rem(me + n - d, n)).wait_recv())
+    unpack(1, proj_ref)
 
     def end_sends(chunk):
         for stage in range(3):
@@ -507,15 +520,16 @@
     def _():
         link_copy(LZ).wait_send()
 
-    around(lambda d: part_copy(d).wait_send())
-    around(lambda d: total_copy(d, me).wait_send())
+    for which in range(2):
+        around(lambda d: part_copy(which, d).wait_send())
+        around(lambda d: total_copy(which, d, me).wait_send())
     result.wait()
 
 
 def per_device(n, vectors, links, rotation):
     count, local_sites = vectors.shape[2], vectors.shape[3]
     chunks = count // CHUNK
-    rows = 8 * -(-8 * count * count // (128 * 8 * n))
+    rows = 8 * -(-(-(-4 * count // 128) * count) // (8 * n))
     all_rows = n * rows
     f32 = jnp.float32
     halo_shape = (2, 3, LZ + 2, count, LAYER)
@@ -544,9 +558,9 @@
             pltpu.VMEM(block, f32),
             pltpu.VMEM(block, f32),
             pltpu.VMEM((4, 2 * count, 2 * count), f32),
-            pltpu.VMEM((all_rows, 128), f32),
-            pltpu.VMEM((n, rows, 128), f32),
-            pltpu.VMEM((all_rows, 128), f32),
+            pltpu.VMEM((2, all_rows, 128), f32),
+            pltpu.VMEM((2, n, rows, 128), f32),
+            pltpu.VMEM((2, all_rows, 128), f32),
             pltpu.SemaphoreType.DMA((LZ,)),
             pltpu.SemaphoreType.DMA((3, 6, chunks)),
             pltpu.SemaphoreType.DMA((3, 6, chunks)),
@@ -554,10 +568,10 @@
             pltpu.SemaphoreType.DMA((LZ + 1,)),
             pltpu.SemaphoreType.DMA((2, chunks)),
             pltpu.SemaphoreType.DMA((2, chunks)),
-            pltpu.SemaphoreType.DMA((n,)),
-            pltpu.SemaphoreType.DMA((n,)),
-            pltpu.SemaphoreType.DMA((n,)),
-            pltpu.SemaphoreType.DMA((n,)),
+            pltpu.SemaphoreType.DMA((2, n)),
+            pltpu.SemaphoreType.DMA((2, n)),
+            pltpu.SemaphoreType.DMA((2, n)),
+            pltpu.SemaphoreType.DMA((2, n)),
             pltpu.VMEM((3, 18, local_sites), f32),
             pltpu.VMEM((2, 2 * count, count), f32),
             pltpu.VMEM(vectors.shape, f32),

time: 113 us -> 113 us (level)
  no operation moved by 1% of the time
where the time goes in v3:
time: 113 us
  Pallas kernels  108 us (96%)
  local copies, waits for them, and re-layouts  3.96 us (4%)
    pallas_call x1, Pallas kernels, per_device(): pl.pallas_call(functools.partial(kernel, n, rows), out_shape=(jax.ShapeDt...  108 us
    unnamed x7, local copies, waits for them, and re-layouts  3.96 us

profile of v3, /device:TPU:0, one launch (start us, length us, event | category | flops | bytes accessed | tf_op | source)
XLA Modules:
  0.0 112.5 jit_solution(4211926486604798076)
XLA Ops:
  0.6 107.9 %shard_map.58 = (f32[2,3,80,768]{3,2,1,0:T(8,128)}, f32[2,160,80]{2,1,0:T(8,128)}, f32[2,160,80]{2,1,0:T(8,128)}) custom-call(f32[2,3,80,768]{3,2,1,0:T(8,128)} %vec_ref.1, f32[3,9,2,768]{3,2,1,0:T(2,128)} %bitcast.1, f32[2,160,160]{2,1,0:T(8,128)} %turn_ref.1), custom_call_target="tpu_custom_call" | custom-call | tf_op jit(solution)/shard_map/pallas_call | solution.py:538
  108.5 0.0 copy-start.1
  108.5 0.0 copy-start
  108.5 2.6 %copy.9 = f32[2,3,80,768]{3,2,1,0:T(8,128)} copy(f32[2,3,80,768]{3,2,1,0:T(8,128)} %get-tuple-element.6) | data formatting | bytes 2949120
  111.2 0.0 copy-done.1
  111.2 0.7 copy.10
  111.8 0.0 copy-done
  111.8 0.7 copy.11
Async XLA Ops:
  108.5 2.6 %copy-start.1 = (f32[2,160,80]{2,1,0:T(8,128)S(1)}, f32[2,160,80]{2,1,0:T(8,128)}, u32[]{:S(2)}) copy-start(f32[2,160,80]{2,1,0:T(8,128)} %get-tuple-element.7) | copy-start | bytes 307204
  108.5 3.3 %copy-start = (f32[2,160,80]{2,1,0:T(8,128)S(1)}, f32[2,160,80]{2,1,0:T(8,128)}, u32[]{:S(2)}) copy-start(f32[2,160,80]{2,1,0:T(8,128)} %get-tuple-element.8) | copy-start | bytes 307204
